TPU v7x, 768 devices: a whole 4x8x12 slice. The times are simulated.
768 devices in a mesh: row: 32 (over x_hi, y, core), col: 24 (over z, x_lo).
Axes of the slice: x: 4 (x_hi: 2, x_lo: 2; x = x_hi * 2 + x_lo), y: 8, z: 12, core: 2. Of those that a mesh axis runs over, the one named last changes fastest.
Arguments:
- design_rows: bfloat16 [768, 12288], P('col', 'row'), may hold values from -1.1953125 to 1.1953125
- design_cols: bfloat16 [768, 24576], P('row', 'col'), may hold values from -1.1953125 to 1.1953125
- whitening: bfloat16 [768, 768], replicated, may hold values from -16 to 16, as said below
- epoch_mask: int32 [128], replicated, may hold values 0 or 1
- normal_old: float32 [12288, 24576], P('row', 'col'), may hold values from -6 to 6
- probes: float32 [24576, 64], P('col'), may hold values from -0.0390625 to 0.0390625
Outputs:
- normal_new: float32 [12288, 24576], P('row', 'col')
- products: float32 [12288, 64], P(('row', 'col'))
Inputs may be any that keep to these rules, and one draw needn't show every extreme that they name: `whitening`: lower triangular with a positive diagonal.
All inputs are finite; a program needn't handle non-finite values.
Results may differ from a plain program's by a relative error of at most 0.0028.
Values may be sent and summed in bfloat16 or wider, within the bound.
A program may use at most 32 MiB of HBM per device.

v0:
```python
import jax
import jax.numpy as jnp
from jax import lax
from jax.sharding import PartitionSpec as P

COMP = 6


def from_everyone(array, axis):
    devices = lax.axis_size(axis)
    return lax.all_to_all(
        jnp.broadcast_to(array[None], (devices, *array.shape)), axis, 0, 0, tiled=True
    )


def laid_out(pieces, dim):
    pieces = jnp.moveaxis(pieces, 0, dim)
    shape = pieces.shape
    return pieces.reshape(*shape[:dim], shape[dim] * shape[dim + 1], *shape[dim + 2 :])


def gather_directly(array, axis, dim):
    pieces = from_everyone(array, axis)
    return laid_out(pieces, dim)


def in_blocks(array, dim, devices):
    shape = array.shape
    pieces = array.reshape(*shape[:dim], devices, shape[dim] // devices, *shape[dim + 1 :])
    return jnp.moveaxis(pieces, dim, 0)


def sent_and_summed(array, axis, dim):
    devices = lax.axis_size(axis)
    pieces = lax.all_to_all(in_blocks(array, dim, devices), axis, 0, 0, tiled=True)
    return jnp.sum(pieces, axis=0)


def body(design_rows, design_cols, whitening, epoch_mask, normal_old, probes):
    obs_mask = jnp.repeat(epoch_mask, COMP).astype(jnp.bfloat16)
    contract = (((0,), (0,)), ((), ()))
    rows_whole = gather_directly(design_rows, "col", 0)
    white_rows = jnp.dot(whitening, rows_whole, preferred_element_type=jnp.float32).astype(
        jnp.bfloat16
    )
    weighted = white_rows * obs_mask[:, None]
    cols_whole = gather_directly(design_cols, "row", 0)
    white_cols = jnp.dot(whitening, cols_whole, preferred_element_type=jnp.float32)
    gram = lax.dot_general(
        weighted.astype(jnp.float32),
        white_cols,
        contract,
        precision=lax.Precision.HIGHEST,
        preferred_element_type=jnp.float32,
    )
    normal_new = normal_old + gram
    partial_sum = jnp.dot(
        normal_new, probes, precision=lax.Precision.HIGHEST, preferred_element_type=jnp.float32
    )
    products = sent_and_summed(partial_sum, "col", 0)
    return (normal_new, products)


def solution(mesh):
    placed = (P("col", "row"), P("row", "col"), P(), P(), P("row", "col"), P("col", None))
    return jax.shard_map(
        body,
        mesh=mesh,
        in_specs=placed,
        out_specs=(P("row", "col"), P(("row", "col"), None)),
        check_vma=False,
    )
```

profile of v0, /device:TPU:8, one launch (start us, length us, event | category | flops | bytes accessed | tf_op | source)
XLA Modules:
  0.0 120.4 jit_solution(2537831230941287835)
XLA Ops:
  0.6 0.0 copy-start
  0.6 0.0 copy-start.5
  0.7 0.9 broadcast_in_dim.6
  1.6 42.3 %all_to_all.15 = bf16[24,32,384]{2,1,0:T(8,128)(2,1)S(1)} all-to-all(bf16[24,32,384]{2,1,0:T(8,128)(2,1)S(1)} %broadcast_in_dim.6), channel_id=1, replica_groups=mesh['row'=32,'col'=24] {'col'}, dimensions={0} | all-to-all | bytes 1179648 | tf_op jit(solution)/shard_map/all_to_all | solution.py:11
  43.9 0.0 copy-done.5
  43.9 1.3 %broadcast_in_dim.8 = bf16[32,24,1024]{2,1,0:T(8,128)(2,1)} broadcast(bf16[24,1024]{1,0:T(8,128)(2,1)S(1)} %copy-done.5), dimensions={1,2} | broadcast | bytes 1622016 | tf_op jit(solution)/shard_map/broadcast_in_dim | solution.py:12
  45.2 0.0 copy-start.6
  45.2 10.0 %all-to-all-start.1 = ((bf16[32,24,1024]{2,1,0:T(8,128)(2,1)}), bf16[32,24,1024]{2,1,0:T(8,128)(2,1)S(1)}, u32[]{:S(2)}, u32[]{:S(2)}) async-start(bf16[32,24,1024]{2,1,0:T(8,128)(2,1)} %broadcast_in_dim.8), calls=%async_computation.1 | async-start | bytes 3145728 | tf_op jit(solution)/shard_map/all_to_all | solution.py:11
  55.2 0.0 copy-done.6
  55.3 0.1 broadcast_in_dim.7
  55.3 0.1 convert_element_type.17
  55.5 0.0 copy-done
  55.5 1.6 %fusion = bf16[768,384]{1,0:T(8,128)(2,1)} fusion(bf16[768,768]{1,0:T(8,128)(2,1)S(1)} %copy-done, bf16[768,384]{1,0:T(8,128)(2,1)S(1)} %bitcast.13, bf16[768]{0:T(1024)(128)(2,1)S(1)} %convert_element_type.17), kind=kOutput, calls=%fused_computation.2 | convolution fusion | flops 453574656 | bytes 2360832 | tf_op jit(solution)/shard_map/dot_general | solution.py:43
  57.1 39.9 %all-to-all-done.1 = bf16[32,24,1024]{2,1,0:T(8,128)(2,1)S(1)} async-done(((bf16[32,24,1024]{2,1,0:T(8,128)(2,1)}), bf16[32,24,1024]{2,1,0:T(8,128)(2,1)S(1)}, u32[]{:S(2)}, u32[]{:S(2)}) %all-to-all-start.1) | async-done | bytes 1572896 | tf_op jit(solution)/shard_map/all_to_all | solution.py:11
  97.0 0.0 copy-start.2
  97.0 0.0 copy-start.3
  97.0 1.4 %fusion.1 = f32[768,1024]{1,0:T(8,128)S(1)} fusion(bf16[768,768]{1,0:T(8,128)(2,1)S(1)} %copy-done, bf16[768,1024]{1,0:T(8,128)(2,1)S(1)} %bitcast.11), kind=kOutput, calls=%fused_computation.3 | convolution fusion | flops 1207959552 | bytes 5898240 | tf_op jit(solution)/shard_map/dot_general | solution.py:48
  98.4 0.0 copy-done.2
  98.4 0.1 copy-done.3
  98.5 0.0 copy-start.4
  98.5 2.2 %convolution_add_fusion = f32[384,1024]{1,0:T(8,128)S(1)} fusion(f32[384,1024]{1,0:T(8,128)S(1)} %copy-done.2, bf16[768,384]{1,0:T(8,128)(2,1)S(1)} %copy-done.3, f32[768,1024]{1,0:T(8,128)S(1)} %fusion.1), kind=kOutput, calls=%fused_computation | convolution fusion | flops 3624271872 | bytes 6881280 | tf_op jit(solution)/shard_map/dot_general | solution.py:49
  100.7 0.0 copy-done.4
  100.7 0.0 copy-start.1
  100.8 1.4 %fusion.2 = f32[384,64]{1,0:T(8,128)S(1)} fusion(f32[384,1024]{1,0:T(8,128)S(1)} %convolution_add_fusion, f32[1024,64]{0,1:T(8,128)S(1)} %copy-done.4), kind=kOutput, calls=%fused_computation.4 | convolution fusion | flops 301989888 | bytes 1933312 | tf_op jit(solution)/shard_map/dot_general | solution.py:57
  102.1 0.2 reshape.25
  102.3 16.0 %all_to_all.16 = f32[24,1,1024]{2,1,0:T(1,128)S(1)} all-to-all(f32[24,1,1024]{2,1,0:T(1,128)S(1)} %reshape.25), channel_id=1, replica_groups=mesh['row'=32,'col'=24] {'col'}, dimensions={0} | all-to-all | bytes 196608 | tf_op jit(solution)/shard_map/all_to_all | solution.py:35
  118.3 0.5 broadcast.3
  118.8 0.9 reduce
  119.6 0.1 reshape.26
  119.7 0.6 reduce_sum.9
  120.4 0.0 copy-done.1
  (1 shorter events, 0.0 us)
Async XLA Ops:
  0.6 54.9 %copy-start = (bf16[768,768]{1,0:T(8,128)(2,1)S(1)}, bf16[768,768]{1,0:T(8,128)(2,1)}, u32[]{:S(2)}) copy-start(bf16[768,768]{1,0:T(8,128)(2,1)} %param.8) | copy-start | bytes 3538948
  0.6 43.2 %copy-start.5 = (bf16[24,1024]{1,0:T(8,128)(2,1)S(1)}, bf16[24,1024]{1,0:T(8,128)(2,1)}, u32[]{:S(2)}) copy-start(bf16[24,1024]{1,0:T(8,128)(2,1)} %param.7) | copy-start | bytes 147460
  45.2 10.0 %copy-start.6 = (s32[128]{0:T(128)S(1)}, s32[128]{0:T(128)}, u32[]{:S(2)}) copy-start(s32[128]{0:T(128)} %param.9) | copy-start | bytes 1540
  45.2 51.7 %all-to-all-start.1 = ((bf16[32,24,1024]{2,1,0:T(8,128)(2,1)}), bf16[32,24,1024]{2,1,0:T(8,128)(2,1)S(1)}, u32[]{:S(2)}, u32[]{:S(2)}) async-start(bf16[32,24,1024]{2,1,0:T(8,128)(2,1)} %broadcast_in_dim.8), calls=%async_computation.1 | async-start | bytes 3145728 | tf_op jit(solution)/shard_map/all_to_all | solution.py:11
  97.0 1.4 %copy-start.2 = (f32[384,1024]{1,0:T(8,128)S(1)}, f32[384,1024]{1,0:T(8,128)}, u32[]{:S(2)}) copy-start(f32[384,1024]{1,0:T(8,128)} %param.10) | copy-start | bytes 4718596
  97.0 1.5 %copy-start.3 = (bf16[768,384]{1,0:T(8,128)(2,1)S(1)}, bf16[768,384]{1,0:T(8,128)(2,1)}, u32[]{:S(2)}) copy-start(bf16[768,384]{1,0:T(8,128)(2,1)} %fusion) | copy-start | bytes 1769476
  98.5 2.2 %copy-start.4 = (f32[1024,64]{0,1:T(8,128)S(1)}, f32[1024,64]{0,1:T(8,128)}, u32[]{:S(2)}) copy-start(f32[1024,64]{0,1:T(8,128)} %param.11) | copy-start | bytes 786436
  100.7 19.6 %copy-start.1 = (f32[384,1024]{1,0:T(8,128)}, f32[384,1024]{1,0:T(8,128)S(1)}, u32[]{:S(2)}) copy-start(f32[384,1024]{1,0:T(8,128)S(1)} %convolution_add_fusion) | copy-start | bytes 4718596
where the time goes:
time: 121 us; the launch traced here: 120 us
  blocking collectives  58.3 us (48%)
  waiting for transfers between devices  39.9 us (33%)
  starting transfers between devices  10 us (8%)
  matrix products  6.57 us (5%)
  local copies, waits for them, and re-layouts  3.4 us (3%)
  other arithmetic  1.51 us (1%)
    all_to_all x1, blocking collectives, from_everyone(): lax.all_to_all(jnp.broadcast_to(array[None], (devices, *array.shape)), ax...  42.3 us
    all_to_all x1, waiting for transfers between devices, from_everyone(): lax.all_to_all(jnp.broadcast_to(array[None], (devices, *array.shape)), ax...  39.9 us
    all_to_all x1, blocking collectives, sent_and_summed(): lax.all_to_all(in_blocks(array, dim, devices), axis, 0, 0, tiled=True)  16 us
    all_to_all x1, starting transfers between devices, from_everyone(): lax.all_to_all(jnp.broadcast_to(array[None], (devices, *array.shape)), ax...  10 us
  transfers between devices with their start and end apart: 1, of which 1 were waited for; matrix products, arithmetic and copies ran while one was open for 2% of the time, Pallas kernels for 0%

commit v1 on v0

v1 whole, which is shorter than its diff:
```python
import jax
import jax.numpy as jnp
from jax import lax
from jax.experimental import pallas as pl
from jax.experimental.pallas import tpu as pltpu
from jax.sharding import PartitionSpec as P

MESH = pl.DeviceIdType.MESH
COMP = 6
NZ, NY = 12, 8
BF, F32 = jnp.bfloat16, jnp.float32


def split2(x):
    hi = x.astype(BF)
    return hi, (x - hi.astype(F32)).astype(BF)


def dot(a, b, dims=((1,), (0,))):
    return lax.dot_general(a, b, (dims, ((), ())), preferred_element_type=F32)


class Names(dict):
    def __missing__(self, key):
        self[key] = len(self)
        return self[key]


def kernel(
    rows_h, cols_h, w_h, mask_v, old_h, prob_h, new_o, prod_o,
    R, RT, C, W, Wm, Y, OLD, PR, PB, PX, Q, G, ss, rs, ls,
):
    row, col = lax.axis_index("row"), lax.axis_index("col")
    core, y, xh = row % 2, (row // 2) % NY, row // (2 * NY)
    z, xl = col // 2, col % 2

    def at_z(k):
        return (z + k + NZ) % NZ

    def at_y(k):
        return (y + k + NY) % NY

    def to_z(k):
        return (row, at_z(k) * 2 + xl)

    def to_y(k):
        return ((xh * NY + at_y(k)) * 2 + core, col)

    to_xl = (row, z * 2 + 1 - xl)
    to_xh = (((1 - xh) * NY + y) * 2 + core, col)
    to_core = ((xh * NY + y) * 2 + 1 - core, col)

    local = [
        pltpu.make_async_copy(src, dst, ls.at[i])
        for i, (src, dst) in enumerate(
            (
                (rows_h, R.at[z, xl]),
                (cols_h, C.at[xh, y, core]),
                (w_h, W),
                (prob_h, PR),
                (old_h, OLD),
            )
        )
    ]
    for copy in local:
        copy.start()

    barrier = pltpu.get_barrier_semaphore()
    others = [to_z(k) for k in range(-5, 7) if k] + [to_y(k) for k in (-2, -1, 1, 2)] + [to_xl, to_xh, to_core]
    for other in others:
        pl.semaphore_signal(barrier, inc=1, device_id=other, device_id_type=MESH)
    pl.semaphore_wait(barrier, len(others))

    sems, sent = Names(), []

    def send(src, dst, name, device):
        copy = pltpu.make_async_remote_copy(
            src_ref=src,
            dst_ref=dst,
            send_sem=ss.at[len(sent)],
            recv_sem=rs.at[sems[name]],
            device_id=device,
            device_id_type=MESH,
        )
        copy.start()
        sent.append(copy)

    def arrive(dst, name):
        pltpu.make_async_remote_copy(
            src_ref=dst, dst_ref=dst, send_sem=ss.at[0], recv_sem=rs.at[sems[name]],
            device_id=to_core, device_id_type=MESH,
        ).wait_recv()

    def rbuf(k, side):
        return R.at[at_z(k), xl if side == 0 else 1 - xl]

    def relay_rows(k, side):
        s = 1 if k > 0 else -1
        buf = rbuf(k, side)
        send(buf, buf, ("r", 4 * s, side), to_z(-s))
        send(buf, buf, ("r", 5 * s, side), to_z(-2 * s))
        half = R.at[at_z(k), xl if side == 0 else 1 - xl, pl.ds(0 if s > 0 else 16, 16)]
        send(half, half, ("r", 6 * s, side), to_z(-3 * s))

    def rows_in(k, side):
        if k == 6:
            for s in (1, -1):
                half = R.at[at_z(k), xl if side == 0 else 1 - xl, pl.ds(0 if s > 0 else 16, 16)]
                arrive(half, ("r", 6 * s, side))
        else:
            arrive(rbuf(k, side), ("r", k, side))

    def cbuf(k, side, sibling=False):
        return C.at[xh if side == 0 else 1 - xh, at_y(k), 1 - core if sibling else core]

    def chalf(k, side, s):
        return C.at[xh if side == 0 else 1 - xh, at_y(k), core, :, pl.ds(0 if s > 0 else 512, 512)]

    def relay_cols(k, side):
        s = 1 if k > 0 else -1
        buf = cbuf(k, side)
        send(buf, buf, ("c", 3 * s, side), to_y(-s))
        half = chalf(k, side, s)
        send(half, half, ("c", 4 * s, side), to_y(-2 * s))

    def cols_in(k, side):
        if k == 4:
            for s in (1, -1):
                arrive(chalf(k, side, s), ("c", 4 * s, side))
        else:
            arrive(cbuf(k, side), ("c", k, side))

    def to_sibling(k, side):
        buf = cbuf(k, side)
        send(buf, buf, ("s", k, side), to_core)

    def from_sibling(k, side):
        arrive(cbuf(k, side, True), ("s", k, side))

    def cross_rows(k):
        buf = rbuf(k, 0)
        send(buf, buf, ("r", k, 1), to_xl)

    def cross_cols(k):
        buf = cbuf(k, 0)
        send(buf, buf, ("c", k, 1), to_xh)

    own_r, own_c = R.at[z, xl], C.at[xh, y, core]
    for k in (3, -3, 2, -2, 1, -1):
        if abs(k) == 2:
            send(cols_h, own_c, ("c", -k, 0), to_y(k))
        if abs(k) == 1:
            send(cols_h, own_c, ("c", -k, 0), to_y(k))
        send(rows_h, own_r, ("r", -k, 0), to_z(k))
    send(cols_h, own_c, ("c", 0, 1), to_xh)
    send(rows_h, own_r, ("r", 0, 1), to_xl)
    send(cols_h, own_c, ("s", 0, 0), to_core)

    for copy in local[2:4]:
        copy.wait()
    obs = lax.broadcasted_iota(jnp.int32, (768, 128), 0)
    first = COMP * lax.broadcasted_iota(jnp.int32, (768, 128), 1)
    keep = (obs >= first) & (obs < first + COMP)
    mask = jnp.sum(jnp.where(keep, mask_v[...].astype(F32), 0.0), axis=1, keepdims=True)
    Wm[...] = W[...] * mask.astype(BF)

    for k in (1, -1):
        rows_in(k, 0)
        cross_rows(k)
    for k in (2, -2):
        cols_in(k, 0)
        relay_cols(k, 0)
        cross_cols(k)
    for k in (3, -3):
        rows_in(k, 0)
        relay_rows(k, 0)
        cross_rows(k)
    for k in (1, -1):
        cols_in(k, 0)
        cross_cols(k)
    for k in (2, -2):
        rows_in(k, 0)
        cross_rows(k)
    cols_in(0, 1)
    for k in (1, -1, 2, -2):
        to_sibling(k, 0)
    to_sibling(0, 1)
    for k in (2, -2):
        cols_in(k, 1)
        relay_cols(k, 1)
    for k in (3, -3):
        rows_in(k, 1)
        relay_rows(k, 1)
    for k in (1, -1):
        cols_in(k, 1)
    for k in (1, -1, 2, -2):
        to_sibling(k, 1)
    for k in (3, -3, 4):
        cols_in(k, 0)
        to_sibling(k, 0)
    for k in (0, 1, -1, 2, -2):
        rows_in(k, 1)
    for side in (0, 1):
        for k in (4, -4, 5, -5, 6):
            rows_in(k, side)
    local[0].wait()
    local[1].wait()
    local[4].wait()

    for b in range(6):
        block = R[2 * b : 2 * b + 2].reshape(128, 384)
        RT[:, 128 * b : 128 * b + 128] = block.T
    white = dot(RT[...], W[...], ((1,), (1,))).astype(BF)
    full = dot(white, Wm[...])
    hi, lo = split2(full)
    for h in range(2):
        Y[h, :384] = hi[:, 384 * h : 384 * h + 384]
        Y[h, 384:] = lo[:, 384 * h : 384 * h + 384]

    def gram(h):
        def tile(n, _):
            at = pl.ds(pl.multiple_of(n * 256, 256), 256)
            cols = C[h, :, :, :, at].reshape(384, 256)
            both = dot(Y[h], cols)
            OLD[:, at] = OLD[:, at] + (both[:384] + both[384:])
            return 0

        lax.fori_loop(0, 4, tile, 0)

    for k in (0, 1, -1, 2, -2, 3, -3, 4):
        from_sibling(k, 0)
    gram(xh)
    for k in (3, -3, 4):
        cols_in(k, 1)
        to_sibling(k, 1)
    for k in (0, 1, -1, 2, -2, 3, -3, 4):
        from_sibling(k, 1)
    gram(1 - xh)

    new = OLD[...]
    new_o[...] = new
    hi, lo = split2(new)
    phi, plo = split2(PR[...])
    both = jnp.concatenate([phi, plo], axis=0)
    part = dot(hi, both, ((1,), (1,)))
    low = dot(lo, phi, ((1,), (1,)))
    part = part[:, :64] + part[:, 64:] + low
    part = part.reshape(48, 8, 64).reshape(24, 2, 8, 64)
    PB[...] = jnp.concatenate([part[:, 0], part[:, 1]], axis=-1).reshape(NZ, 2, 8, 128)

    send(PB.at[:, 1 - xl], PX, ("px",), to_xl)
    arrive(PX, ("px",))
    Q[...] = PB[:, xl] + PX[...]
    for k in (6, 5, -5, 4, -4, 3, -3, 2, -2, 1, -1):
        send(Q.at[at_z(k)], G.at[k + 5], ("q", k), to_z(k))
    total = Q[z]
    for k in (1, -1, 2, -2, 3, -3, 4, -4, 5, -5, 6):
        arrive(G.at[k + 5], ("q", k))
        total = total + G[k + 5]
    prod_o[:8] = total[:, :64]
    prod_o[8:] = total[:, 64:]
    for copy in sent:
        copy.wait_send()


def body(design_rows, design_cols, whitening, epoch_mask, normal_old, probes):
    vmem = pl.BlockSpec(memory_space=pltpu.VMEM)
    hbm = pl.BlockSpec(memory_space=pl.ANY)
    return pl.pallas_call(
        kernel,
        out_shape=(
            jax.ShapeDtypeStruct((384, 1024), F32),
            jax.ShapeDtypeStruct((16, 64), F32),
        ),
        in_specs=[hbm, hbm, hbm, vmem, hbm, hbm],
        out_specs=(vmem, vmem),
        scratch_shapes=[
            pltpu.VMEM((NZ, 2, 32, 384), BF),
            pltpu.VMEM((384, 768), BF),
            pltpu.VMEM((2, NY, 2, 24, 1024), BF),
            pltpu.VMEM((768, 768), BF),
            pltpu.VMEM((768, 768), BF),
            pltpu.VMEM((2, 768, 384), BF),
            pltpu.VMEM((384, 1024), F32),
            pltpu.VMEM((64, 1024), F32),
            pltpu.VMEM((NZ, 2, 8, 128), F32),
            pltpu.VMEM((NZ, 8, 128), F32),
            pltpu.VMEM((NZ, 8, 128), F32),
            pltpu.VMEM((NZ, 8, 128), F32),
            pltpu.SemaphoreType.DMA((96,)),
            pltpu.SemaphoreType.DMA((96,)),
            pltpu.SemaphoreType.DMA((5,)),
        ],
        compiler_params=pltpu.CompilerParams(
            collective_id=0, has_side_effects=True, vmem_limit_bytes=48 * 2**20
        ),
        name="normal_update",
    )(
        design_rows,
        design_cols,
        whitening,
        epoch_mask.reshape(1, 128),
        normal_old,
        probes.T,
    )


def solution(mesh):
    placed = (P("col", "row"), P("row", "col"), P(), P(), P("row", "col"), P("col", None))
    return jax.shard_map(
        body,
        mesh=mesh,
        in_specs=placed,
        out_specs=(P("row", "col"), P(("row", "col"), None)),
        check_vma=False,
    )
```

time: 121 us -> 59 us (0.49)
  the two profiles are of different devices: /device:TPU:8 before, /device:TPU:1 now
where the time goes in v1:
time: 59 us; the launch traced here: 58.6 us
  Pallas kernels  50.4 us (85%)
  local copies, waits for them, and re-layouts  7.55 us (13%)
  between operations  0.65 us (1%)
    pallas_call x1, Pallas kernels, body(): pl.pallas_call(kernel, out_shape=(jax.ShapeDtypeStruct((384, 1024), F32),...  50.4 us
    unnamed x14, local copies, waits for them, and re-layouts  7.55 us

profile of v1, /device:TPU:1, one launch (start us, length us, event | category | flops | bytes accessed | tf_op | source)
XLA Modules:
  0.0 58.6 jit_solution(15746679944188052980)
XLA Ops:
  0.6 0.0 copy-start
  0.6 1.4 %copy-done = f32[384,1024]{1,0:T(8,128)S(1)} copy-done((f32[384,1024]{1,0:T(8,128)S(1)}, f32[384,1024]{1,0:T(8,128)}, u32[]{:S(2)}) %copy-start) | copy-done | bytes 1572888
  2.0 0.0 copy-start.1
  2.0 1.3 %copy-done.1 = bf16[768,768]{1,0:T(8,128)(2,1)S(1)} copy-done((bf16[768,768]{1,0:T(8,128)(2,1)S(1)}, bf16[768,768]{1,0:T(8,128)(2,1)}, u32[]{:S(2)}) %copy-start.1) | copy-done | bytes 1179672
  3.3 0.0 copy-start.2
  3.3 0.9 %copy-done.2 = f32[1024,64]{0,1:T(8,128)S(1)} copy-done((f32[1024,64]{0,1:T(8,128)S(1)}, f32[1024,64]{0,1:T(8,128)}, u32[]{:S(2)}) %copy-start.2) | copy-done | bytes 262168
  4.3 0.0 copy-start.3
  4.3 0.8 %copy-done.3 = bf16[24,1024]{1,0:T(8,128)(2,1)S(1)} copy-done((bf16[24,1024]{1,0:T(8,128)(2,1)S(1)}, bf16[24,1024]{1,0:T(8,128)(2,1)}, u32[]{:S(2)}) %copy-start.3) | copy-done | bytes 49176
  5.1 0.0 copy-start.4
  5.1 0.7 %copy-done.4 = bf16[32,384]{1,0:T(8,128)(2,1)S(1)} copy-done((bf16[32,384]{1,0:T(8,128)(2,1)S(1)}, bf16[32,384]{1,0:T(8,128)(2,1)}, u32[]{:S(2)}) %copy-start.4) | copy-done | bytes 24600
  5.8 0.0 copy-start.5
  5.8 0.7 %copy-done.5 = s32[128]{0:T(128)S(1)} copy-done((s32[128]{0:T(128)S(1)}, s32[128]{0:T(128)}, u32[]{:S(2)}) %copy-start.5) | copy-done | bytes 536
  6.5 50.4 %normal_update.1 = (f32[384,1024]{1,0:T(8,128)S(1)}, f32[16,64]{1,0:T(8,128)S(1)}) custom-call(bf16[32,384]{1,0:T(8,128)(2,1)S(1)} %copy-done.4, bf16[24,1024]{1,0:T(8,128)(2,1)S(1)} %copy-done.3, bf16[768,768]{1,0:T(8,128)(2,1)S(1)} %copy-done.1, s32[1,128]{1,0:T(1,128)S(1)} %bitcast.3, f32[384,1024]{1,0:T(8,128)S(1)} %copy-done, f32[64,1024]{1,0:T(8,128)S(1)} %bitcast.2), custom_call_target="tpu_custom_call" | custom-call | tf_op jit(solution)/shard_map/normal_update/pallas_call | solution.py:269
  56.9 1.1 %copy.10 = f32[384,1024]{1,0:T(8,128)} copy(f32[384,1024]{1,0:T(8,128)S(1)} %get-tuple-element.4) | data formatting | bytes 3145728
  58.0 0.6 %copy.11 = f32[16,64]{1,0:T(8,128)} copy(f32[16,64]{1,0:T(8,128)S(1)} %get-tuple-element.5) | data formatting | bytes 8192
Async XLA Ops:
  0.6 1.4 %copy-start = (f32[384,1024]{1,0:T(8,128)S(1)}, f32[384,1024]{1,0:T(8,128)}, u32[]{:S(2)}) copy-start(f32[384,1024]{1,0:T(8,128)} %old_h.1) | copy-start | bytes 4718596
  2.0 1.3 %copy-start.1 = (bf16[768,768]{1,0:T(8,128)(2,1)S(1)}, bf16[768,768]{1,0:T(8,128)(2,1)}, u32[]{:S(2)}) copy-start(bf16[768,768]{1,0:T(8,128)(2,1)} %w_h.1) | copy-start | bytes 3538948
  3.3 0.9 %copy-start.2 = (f32[1024,64]{0,1:T(8,128)S(1)}, f32[1024,64]{0,1:T(8,128)}, u32[]{:S(2)}) copy-start(f32[1024,64]{0,1:T(8,128)} %param.11) | copy-start | bytes 786436
  4.3 0.8 %copy-start.3 = (bf16[24,1024]{1,0:T(8,128)(2,1)S(1)}, bf16[24,1024]{1,0:T(8,128)(2,1)}, u32[]{:S(2)}) copy-start(bf16[24,1024]{1,0:T(8,128)(2,1)} %cols_h.1) | copy-start | bytes 147460
  5.1 0.7 %copy-start.4 = (bf16[32,384]{1,0:T(8,128)(2,1)S(1)}, bf16[32,384]{1,0:T(8,128)(2,1)}, u32[]{:S(2)}) copy-start(bf16[32,384]{1,0:T(8,128)(2,1)} %rows_h.1) | copy-start | bytes 73732
  5.8 0.7 %copy-start.5 = (s32[128]{0:T(128)S(1)}, s32[128]{0:T(128)}, u32[]{:S(2)}) copy-start(s32[128]{0:T(128)} %param.9) | copy-start | bytes 1540

commit v2 on v1

v2 whole, which is shorter than its diff:
```python
import jax
import jax.numpy as jnp
from jax import lax
from jax.experimental import pallas as pl
from jax.experimental.pallas import tpu as pltpu
from jax.sharding import PartitionSpec as P

MESH = pl.DeviceIdType.MESH
COMP = 6
NZ, NY = 12, 8
BF, F32 = jnp.bfloat16, jnp.float32


def split2(x):
    hi = x.astype(BF)
    return hi, (x - hi.astype(F32)).astype(BF)


def dot(a, b, dims=((1,), (0,))):
    return lax.dot_general(a, b, (dims, ((), ())), preferred_element_type=F32)


def pack(x):
    return jnp.concatenate(split2(x), axis=-1)


def unpack(x):
    x = x.astype(F32)
    return x[..., :64] + x[..., 64:]


class Names(dict):
    def __missing__(self, key):
        self[key] = len(self)
        return self[key]


def kernel(
    rows_h, cols_h, w_h, mask_v, old_h, prob_h, new_o, prod_o,
    R, RT, C, W, Wm, Y, OLD, PR, PB, PX, Q, QB, QR, GX, GS, GZ, GF, ss, rs, ls,
):
    row, col = lax.axis_index("row"), lax.axis_index("col")
    core, y, xh = row % 2, (row // 2) % NY, row // (2 * NY)
    z, xl = col // 2, col % 2

    def at_z(k):
        return (z + k + NZ) % NZ

    def at_y(k):
        return (y + k + NY) % NY

    def to_z(k):
        return (row, at_z(k) * 2 + xl)

    def to_y(k):
        return ((xh * NY + at_y(k)) * 2 + core, col)

    other_row = ((1 - xh) * NY + y) * 2 + core
    to_xl = (row, z * 2 + 1 - xl)
    to_xh = (other_row, col)
    to_diagonal = (other_row, z * 2 + 1 - xl)
    to_core = ((xh * NY + y) * 2 + 1 - core, col)

    barrier = pltpu.get_barrier_semaphore()
    others = [to_z(k) for k in range(-5, 7) if k] + [to_y(k) for k in range(-3, 5) if k]
    others += [to_xl, to_xh, to_diagonal, to_core]
    for other in others:
        pl.semaphore_signal(barrier, inc=1, device_id=other, device_id_type=MESH)

    local = [
        pltpu.make_async_copy(src, dst, ls.at[i])
        for i, (src, dst) in enumerate(
            (
                (cols_h, C.at[xh, y, core]),
                (prob_h, PR),
                (rows_h, R.at[z, xl]),
                (w_h, W),
                (old_h, OLD),
            )
        )
    ]
    for copy in local:
        copy.start()
    pl.semaphore_wait(barrier, len(others))

    sems, sent = Names(), []

    def send(src, dst, name, device):
        copy = pltpu.make_async_remote_copy(
            src_ref=src,
            dst_ref=dst,
            send_sem=ss.at[len(sent)],
            recv_sem=rs.at[sems[name]],
            device_id=device,
            device_id_type=MESH,
        )
        copy.start()
        sent.append(copy)

    def arrive(dst, name):
        pltpu.make_async_remote_copy(
            src_ref=dst, dst_ref=dst, send_sem=ss.at[0], recv_sem=rs.at[sems[name]],
            device_id=to_core, device_id_type=MESH,
        ).wait_recv()

    def rbuf(k, side):
        return R.at[at_z(k), xl if side == 0 else 1 - xl]

    def rhalf(k, side, s):
        return R.at[at_z(k), xl if side == 0 else 1 - xl, pl.ds(0 if s > 0 else 16, 16)]

    def relay_rows(k, side):
        s = 1 if k > 0 else -1
        buf, half = rbuf(k, side), rhalf(k, side, s)
        send(half, half, ("r", 6 * s, side), to_z(-3 * s))
        send(buf, buf, ("r", 5 * s, side), to_z(-2 * s))
        send(buf, buf, ("r", 4 * s, side), to_z(-s))

    def rows_in(k, side):
        if k == 6:
            for s in (1, -1):
                arrive(rhalf(k, side, s), ("r", 6 * s, side))
        else:
            arrive(rbuf(k, side), ("r", k, side))

    def cbuf(k, side, sibling=False):
        return C.at[xh if side == 0 else 1 - xh, at_y(k), 1 - core if sibling else core]

    def chalf(k, side, s):
        return C.at[xh if side == 0 else 1 - xh, at_y(k), core, :, pl.ds(0 if s > 0 else 512, 512)]

    def relay_cols(k, side):
        s = 1 if k > 0 else -1
        buf, half = cbuf(k, side), chalf(k, side, s)
        send(half, half, ("c", 4 * s, side), to_y(-2 * s))
        send(buf, buf, ("c", 3 * s, side), to_y(-s))

    def cols_in(k, side):
        if k == 4:
            for s in (1, -1):
                arrive(chalf(k, side, s), ("c", 4 * s, side))
        else:
            arrive(cbuf(k, side), ("c", k, side))

    def to_sibling(k, side):
        buf = cbuf(k, side)
        send(buf, buf, ("s", k, side), to_core)

    def from_sibling(k, side):
        arrive(cbuf(k, side, True), ("s", k, side))

    def cross_rows(k):
        buf = rbuf(k, 0)
        send(buf, buf, ("r", k, 1), to_xl)

    def cross_cols(k):
        buf = cbuf(k, 0)
        send(buf, buf, ("c", k, 1), to_xh)

    own_r, own_c = R.at[z, xl], C.at[xh, y, core]
    send(rows_h, own_r, ("r", -3, 0), to_z(3))
    send(rows_h, own_r, ("r", 3, 0), to_z(-3))
    send(cols_h, own_c, ("c", -2, 0), to_y(2))
    send(cols_h, own_c, ("c", 2, 0), to_y(-2))
    send(cols_h, own_c, ("c", 0, 1), to_xh)
    send(rows_h, own_r, ("r", 0, 1), to_xl)
    for k in (1, -1):
        send(cols_h, own_c, ("c", -k, 0), to_y(k))
        send(rows_h, own_r, ("r", -k, 0), to_z(k))
    for k in (2, -2):
        send(rows_h, own_r, ("r", -k, 0), to_z(k))
    send(cols_h, own_c, ("s", 0, 0), to_core)

    local[0].wait()
    local[1].wait()
    phi, plo = split2(PR[...])
    both = jnp.concatenate([phi, plo], axis=0)
    share = unpack(dot(C[xh, y, core], both, ((1,), (1,))))
    GS[0, 0] = pack(share)
    for i, device in enumerate((to_xl, to_xh, to_diagonal)):
        send(GS.at[0, 0], GX.at[i], ("gx", i), device)

    local[3].wait()
    obs = lax.broadcasted_iota(jnp.int32, (768, 128), 0)
    first = COMP * lax.broadcasted_iota(jnp.int32, (768, 128), 1)
    keep = (obs >= first) & (obs < first + COMP)
    mask = jnp.sum(jnp.where(keep, mask_v[...].astype(F32), 0.0), axis=1, keepdims=True)
    Wm[...] = W[...] * mask.astype(BF)

    for k in (1, -1):
        rows_in(k, 0)
        cross_rows(k)
    for k in (2, -2):
        cols_in(k, 0)
        relay_cols(k, 0)
        cross_cols(k)
    for k in (3, -3):
        rows_in(k, 0)
        relay_rows(k, 0)
        cross_rows(k)

    for i in range(3):
        arrive(GX.at[i], ("gx", i))
    mine = share + unpack(GX[0])
    theirs = unpack(GX[1]) + unpack(GX[2])
    GS[1, 0] = pack(mine)
    GS[1, 1] = pack(theirs)
    for i, k in enumerate((1, -1)):
        send(GS.at[1], GZ.at[i], ("gz", i), to_z(k))

    for k in (1, -1):
        cols_in(k, 0)
        cross_cols(k)
    for k in (2, -2):
        rows_in(k, 0)
        cross_rows(k)
    cols_in(0, 1)
    for k in (2, -2, 1, -1):
        to_sibling(k, 0)
    to_sibling(0, 1)

    local[4].wait()
    hi, lo = split2(OLD[...])
    PB[...] = pack(unpack(dot(hi, both, ((1,), (1,)))) + dot(lo, phi, ((1,), (1,)))).reshape(NZ, 2, 16, 128)
    send(PB.at[:, 1 - xl], PX, ("px",), to_xl)

    for i in range(2):
        arrive(GZ.at[i], ("gz", i))
        mine = mine + unpack(GZ[i, 0])
        theirs = theirs + unpack(GZ[i, 1])
    GS[2, 0] = pack(mine)
    GS[2, 1] = pack(theirs)
    for i, k in enumerate((6, 3, -3)):
        send(GS.at[2], GZ.at[2 + i], ("gz", 2 + i), to_z(k))

    for k in (3, -3):
        rows_in(k, 1)
        relay_rows(k, 1)
    for k in (2, -2):
        cols_in(k, 1)
        relay_cols(k, 1)

    arrive(PX, ("px",))
    Q[...] = unpack(PB[:, xl]) + unpack(PX[...])
    QB[...] = pack(Q[...])
    for k in (6, 5, -5, 4, -4, 3, -3, 2, -2, 1, -1):
        send(QB.at[at_z(k)], QR.at[k + 5], ("q", k), to_z(k))

    for k in (2, -2):
        to_sibling(k, 1)
    for k in (3, -3, 4):
        cols_in(k, 0)
        to_sibling(k, 0)
    for k in (1, -1):
        cols_in(k, 1)
        to_sibling(k, 1)

    def turn(j):
        pair = (z // 2 + j + 6) % 6
        block = R[pl.ds(2 * pair, 2)].reshape(128, 384)
        RT[:, pl.ds(pl.multiple_of(128 * pair, 128), 128)] = block.T

    local[2].wait()
    for k in (0, 1, -1, 2, -2):
        rows_in(k, 1)
    for j in (0, 1, -1):
        turn(j)

    for i in range(2, 5):
        arrive(GZ.at[i], ("gz", i))
        mine = mine + unpack(GZ[i, 0])
        theirs = theirs + unpack(GZ[i, 1])
    GF[xh, y, core] = pack(mine)
    GF[1 - xh, y, core] = pack(theirs)
    for k in (4, 3, -3, 2, -2, 1, -1):
        send(GF.at[:, y, core], GF.at[:, y, core], ("gf", k), to_y(k))

    for side in (0, 1):
        for k in (4, -4, 5, -5, 6):
            rows_in(k, side)
    for j in (2, -2, 3):
        turn(j)

    parts = []
    for b in range(3):
        end = 256 * b + 256
        parts.append(dot(RT[:, :end], W[256 * b : end, :end], ((1,), (1,))).astype(BF))
    white = jnp.concatenate(parts, axis=1)
    parts = [dot(white[:, 256 * b :], Wm[256 * b :, 256 * b : 256 * b + 256]) for b in range(3)]
    hi, lo = split2(jnp.concatenate(parts, axis=1))
    for h in range(2):
        Y[h, :384] = hi[:, 384 * h : 384 * h + 384]
        Y[h, 384:] = lo[:, 384 * h : 384 * h + 384]

    def gram(h, old, new):
        def tile(n, _):
            at = pl.ds(pl.multiple_of(n * 256, 256), 256)
            both = dot(Y[h], C[h, :, :, :, at].reshape(384, 256))
            new[:, at] = old[:, at] + (both[:384] + both[384:])
            return 0

        lax.fori_loop(0, 4, tile, 0)

    for k in (0, 1, -1, 2, -2, 3, -3, 4):
        from_sibling(k, 0)
    for k in (3, -3, 4):
        cols_in(k, 1)
        to_sibling(k, 1)
    gram(xh, OLD, OLD)
    for k in (4, 3, -3, 2, -2, 1, -1):
        arrive(GF.at[:, at_y(-k), core], ("gf", k))
    send(GF.at[:, :, core], GF.at[:, :, core], ("gs",), to_core)
    for k in (0, 1, -1, 2, -2, 3, -3, 4):
        from_sibling(k, 1)
    gram(1 - xh, OLD, new_o)

    total = jnp.zeros((16, 128), F32)
    for k in (1, -1, 2, -2, 3, -3, 4, -4, 5, -5, 6):
        arrive(QR.at[k + 5], ("q", k))
        total = total + QR[k + 5].astype(F32)
    total = Q[z] + unpack(total)
    arrive(GF.at[:, :, 1 - core], ("gs",))
    for h in range(2):
        at = pl.multiple_of(col * 16, 16)
        for first in (0, 384):
            total = total + unpack(dot(Y[h, pl.ds(first + at, 16)], GF[h].reshape(384, 128)))
    prod_o[...] = total
    for copy in sent:
        copy.wait_send()


def write_out(new_v, prod_v, new_h, prod_h, sems):
    copies = [pltpu.make_async_copy(prod_v, prod_h, sems.at[4])]
    for i in range(4):
        rows = pl.ds(96 * i, 96)
        copies.append(pltpu.make_async_copy(new_v.at[rows], new_h.at[rows], sems.at[i]))
    for copy in copies:
        copy.start()
    for copy in copies:
        copy.wait()


def body(design_rows, design_cols, whitening, epoch_mask, normal_old, probes):
    vmem = pl.BlockSpec(memory_space=pltpu.VMEM)
    hbm = pl.BlockSpec(memory_space=pltpu.HBM)
    new, products = pl.pallas_call(
        kernel,
        out_shape=(pltpu.VMEM((384, 1024), F32), pltpu.VMEM((16, 64), F32)),
        in_specs=[hbm, hbm, hbm, vmem, hbm, hbm],
        out_specs=(vmem, vmem),
        scratch_shapes=[
            pltpu.VMEM((NZ, 2, 32, 384), BF),
            pltpu.VMEM((384, 768), BF),
            pltpu.VMEM((2, NY, 2, 24, 1024), BF),
            pltpu.VMEM((768, 768), BF),
            pltpu.VMEM((768, 768), BF),
            pltpu.VMEM((2, 768, 384), BF),
            pltpu.VMEM((384, 1024), F32),
            pltpu.VMEM((64, 1024), F32),
            pltpu.VMEM((NZ, 2, 16, 128), BF),
            pltpu.VMEM((NZ, 16, 128), BF),
            pltpu.VMEM((NZ, 16, 64), F32),
            pltpu.VMEM((NZ, 16, 128), BF),
            pltpu.VMEM((NZ, 16, 128), BF),
            pltpu.VMEM((3, 24, 128), BF),
            pltpu.VMEM((3, 2, 24, 128), BF),
            pltpu.VMEM((5, 2, 24, 128), BF),
            pltpu.VMEM((2, NY, 2, 24, 128), BF),
            pltpu.SemaphoreType.DMA((112,)),
            pltpu.SemaphoreType.DMA((112,)),
            pltpu.SemaphoreType.DMA((5,)),
        ],
        compiler_params=pltpu.CompilerParams(
            collective_id=0, has_side_effects=True, vmem_limit_bytes=56 * 2**20
        ),
        name="normal_update",
    )(
        design_rows,
        design_cols,
        whitening,
        epoch_mask.reshape(1, 128),
        normal_old,
        probes.T,
    )
    return pl.pallas_call(
        write_out,
        out_shape=(
            jax.ShapeDtypeStruct((384, 1024), F32),
            jax.ShapeDtypeStruct((16, 64), F32),
        ),
        in_specs=[vmem, vmem],
        out_specs=(hbm, hbm),
        scratch_shapes=[pltpu.SemaphoreType.DMA((5,))],
        compiler_params=pltpu.CompilerParams(vmem_limit_bytes=4 * 2**20),
        name="write_out",
    )(new, products)


def solution(mesh):
    placed = (P("col", "row"), P("row", "col"), P(), P(), P("row", "col"), P("col", None))
    return jax.shard_map(
        body,
        mesh=mesh,
        in_specs=placed,
        out_specs=(P("row", "col"), P(("row", "col"), None)),
        check_vma=False,
    )
```

time: 59 us -> 45.8 us (0.78)
  local copies, waits for them, and re-layouts: 7.55 us -> 0 us
  Pallas kernels: 50.4 us -> 45 us
    unnamed x14 -> x0, local copies, waits for them, and re-layouts: 7.55 us -> none
    pallas_call x1 -> x2, Pallas kernels: 50.4 us -> 45 us  [the longest x1 43.8 us: body(): pl.pallas_call(kernel, out_shape=(pltpu.VMEM((384, 1024), F32), pltpu.VME...]
where the time goes in v2:
time: 45.8 us; the launch traced here: 45.6 us
  Pallas kernels  45 us (98%)
  between operations  0.64 us (1%)
    pallas_call x1, Pallas kernels, body(): pl.pallas_call(kernel, out_shape=(pltpu.VMEM((384, 1024), F32), pltpu.VME...  43.8 us
    pallas_call x1, Pallas kernels, body(): pl.pallas_call(write_out, out_shape=(jax.ShapeDtypeStruct((384, 1024), F3...  1.18 us

profile of v2, /device:TPU:1, one launch (start us, length us, event | category | flops | bytes accessed | tf_op | source)
XLA Modules:
  0.0 45.6 jit_solution(12512315507831853184)
XLA Ops:
  0.6 43.8 %normal_update.1 = (f32[384,1024]{1,0:T(8,128)S(1)}, f32[16,64]{1,0:T(8,128)S(1)}) custom-call(bf16[32,384]{1,0:T(8,128)(2,1)} %rows_h.1, bf16[24,1024]{1,0:T(8,128)(2,1)} %cols_h.1, bf16[768,768]{1,0:T(8,128)(2,1)} %w_h.1, s32[1,128]{1,0:T(1,128)} %bitcast.3, f32[384,1024]{1,0:T(8,128)} %old_h.1, f32[64,1024]{1,0:T(8,128)} %bitcast.2), custom_call_target="tpu_custom_call" | custom-call | tf_op jit(solution)/shard_map/normal_update/pallas_call | solution.py:346
  44.4 1.2 %write_out.1 = (f32[384,1024]{1,0:T(8,128)}, f32[16,64]{1,0:T(8,128)}) custom-call(f32[384,1024]{1,0:T(8,128)S(1)} %get-tuple-element.4.new_v, f32[16,64]{1,0:T(8,128)S(1)} %get-tuple-element.5.prod_v), custom_call_target="tpu_custom_call" | custom-call | tf_op jit(solution)/shard_map/write_out/pallas_call | solution.py:385

commit v3 on v0

v3 whole, which is shorter than its diff:
```python
import jax
import jax.numpy as jnp
from jax import lax
from jax.experimental import pallas as pl
from jax.experimental.pallas import tpu as pltpu
from jax.sharding import PartitionSpec as P

MESH = pl.DeviceIdType.MESH
COMP = 6
NZ, NY = 12, 8
BF, F32 = jnp.bfloat16, jnp.float32


def split2(x):
    hi = x.astype(BF)
    return hi, (x - hi.astype(F32)).astype(BF)


def dot(a, b, dims=((1,), (0,))):
    return lax.dot_general(a, b, (dims, ((), ())), preferred_element_type=F32)


def pack(x):
    return jnp.concatenate(split2(x), axis=-1)


def unpack(x):
    x = x.astype(F32)
    return x[..., :64] + x[..., 64:]


class Names(dict):
    def __missing__(self, key):
        self[key] = len(self)
        return self[key]


ROWS_ACROSS, ROWS_DIRECT = (3, -3), (2, -2, 1, -1)
COLS_ACROSS, COLS_DIRECT = (2, -2), (1, -1)
FIRST = (
    ("r", 1, 0), ("r", -3, 0), ("r", 3, 0), ("r", -2, 0), ("c", 2, 0), ("c", 1, 0),
    ("c", -2, 0), ("r", 0, 1), ("r", 2, 0), ("r", -1, 0), ("c", 0, 1), ("c", -1, 0),
)
EARLY = 9
ORDER = (
    "g", "mask", "sold0", ("r", 0, 1), "sold1", "sold2",
    "g1", ("c", 1, 0), ("c", -2, 0), ("r", 3, 0), ("c", 2, 0), ("c", -1, 0),
    ("r", -3, 0), ("c", 0, 1), "p1", "g2", ("c", -3, 0), ("r", 3, 1),
    ("c", -2, 1), ("c", 3, 0), ("c", 1, 1), ("c", -1, 1), ("r", -3, 1), ("c", 2, 1),
    "c4_0", "p2b", "turnA", "p2a", ("c", -3, 1), "g3",
    "c4_1", ("c", 3, 1), "turnB", "white0", "white1", "white2",
    "back2", "back1", "back0", "gramA0", "gramA1", "gramA2",
    "gramA3", "gramB0", "gs", "gramB1", "gramB2", "gramB3",
    "psum", "prod",
)


def kernel(
    rows_h, cols_h, w_h, mask_v, old_h, prob_h, new_o, prod_o,
    R, RT, C, W, Wm, WH, Y, OLD, PR, PB, PX, Q, QB, QR, QS, GX, GS, GZ, GF, ss, rs, ls,
):
    row, col = lax.axis_index("row"), lax.axis_index("col")
    core, y, xh = row % 2, (row // 2) % NY, row // (2 * NY)
    z, xl = col // 2, col % 2

    def at_z(k):
        return (z + k + NZ) % NZ

    def at_y(k):
        return (y + k + NY) % NY

    def to_z(k):
        return (row, at_z(k) * 2 + xl)

    def to_y(k):
        return ((xh * NY + at_y(k)) * 2 + core, col)

    other_row = ((1 - xh) * NY + y) * 2 + core
    to_xl = (row, z * 2 + 1 - xl)
    to_xh = (other_row, col)
    to_diagonal = (other_row, z * 2 + 1 - xl)
    to_core = ((xh * NY + y) * 2 + 1 - core, col)

    barrier = pltpu.get_barrier_semaphore()
    others = [to_z(k) for k in (1, -1, 2, -2, 3, -3)] + [to_y(k) for k in (1, -1, 2, -2)]
    others += [to_xl, to_xh, to_diagonal, to_core]
    for other in others:
        pl.semaphore_signal(barrier, inc=1, device_id=other, device_id_type=MESH)

    loads = {
        name: pltpu.make_async_copy(src, dst, ls.at[i])
        for i, (name, src, dst) in enumerate(
            (
                ("cols", cols_h, C.at[xh, y, core]),
                ("probes", prob_h, PR),
                ("rows", rows_h, R.at[z, xl]),
                ("whitening", w_h, W),
                ("old", old_h, OLD),
            )
        )
    }
    for load in loads.values():
        load.start()
    pl.semaphore_wait(barrier, len(others))

    sems, sent, seen = Names(), [], set()

    def send(src, dst, name, device):
        copy = pltpu.make_async_remote_copy(
            src_ref=src,
            dst_ref=dst,
            send_sem=ss.at[len(sent)],
            recv_sem=rs.at[sems[name]],
            device_id=device,
            device_id_type=MESH,
        )
        copy.start()
        sent.append(copy)

    def loaded(name):
        if name not in seen:
            seen.add(name)
            loads[name].wait()

    def place(name):
        kind, k, *side = name
        if kind == "r":
            at = (at_z(k), xl if side[0] == 0 else 1 - xl)
            return R.at[(*at, pl.ds(0 if k > 0 else 16, 16))] if abs(k) == 6 else R.at[at]
        if kind in ("c", "s"):
            at = (xh if side[0] == 0 else 1 - xh, at_y(k), core if kind == "c" else 1 - core)
            if kind == "c" and abs(k) == 4:
                return C.at[(*at, slice(None), pl.ds(0 if k > 0 else 512, 512))]
            return C.at[at]
        if kind == "gx":
            return GX.at[k]
        if kind in ("ga", "gb"):
            return GZ.at[{"ga": {-1: 0, 1: 1, 2: 2}, "gb": {4: 3, -4: 4}}[kind][k]]
        if kind == "gf":
            if abs(k) == 4:
                return GF.at[xh if k > 0 else 1 - xh, at_y(k), core]
            return GF.at[:, at_y(k), core]
        if kind == "gs":
            return GF.at[:, :, 1 - core]
        if kind == "px":
            return PX
        if kind == "qa":
            return QR.at[{4: 0, 5: 1, 6: 2, -4: 3, -5: 4}[k]]
        return QR.at[{1: 5, -1: 6, 2: 7, -2: 8, 3: 9, -3: 10}[k]]

    def need(name):
        if name not in seen:
            seen.add(name)
            ref = place(name)
            pltpu.make_async_remote_copy(
                src_ref=ref, dst_ref=ref, send_sem=ss.at[0], recv_sem=rs.at[sems[name]],
                device_id=to_core, device_id_type=MESH,
            ).wait_recv()

    def buf(kind, k, side):
        if kind == "r":
            return R.at[at_z(k), xl if side == 0 else 1 - xl]
        return C.at[xh if side == 0 else 1 - xh, at_y(k), core]

    def relay_rows(k, side):
        s = 1 if k > 0 else -1
        b = buf("r", k, side)
        half = b.at[pl.ds(0 if s > 0 else 16, 16)]
        send(half, half, ("r", 6 * s, side), to_z(-3 * s))
        send(b, b, ("r", 5 * s, side), to_z(-2 * s))
        send(b, b, ("r", 4 * s, side), to_z(-s))

    def relay_cols(k, side):
        s = 1 if k > 0 else -1
        b = buf("c", k, side)
        half = b.at[:, pl.ds(0 if s > 0 else 512, 512)]
        send(half, half, ("c", 4 * s, side), to_y(-2 * s))
        send(b, b, ("c", 3 * s, side), to_y(-s))

    def to_sibling(k, side):
        b = buf("c", k, side)
        send(b, b, ("s", k, side), to_core)

    def came(name):
        kind, k, side = name
        need(name)
        b = buf(kind, k, side)
        if kind == "r":
            if side == 0 and k in ROWS_ACROSS and abs(k) != 3:
                send(b, b, ("r", k, 1), to_xl)
            if abs(k) == 3:
                relay_rows(k, side)
                if side == 0 and k in ROWS_ACROSS:
                    send(b, b, ("r", k, 1), to_xl)
            if side == 1 and k == 0:
                for d in ROWS_DIRECT:
                    send(b, b, ("r", -d, 1), to_z(d))
        else:
            if side == 0 and k in COLS_ACROSS:
                send(b, b, ("c", k, 1), to_xh)
            if abs(k) == 2:
                relay_cols(k, side)
            if side == 1 and k == 0:
                for d in COLS_DIRECT:
                    send(b, b, ("c", -d, 1), to_y(d))
            to_sibling(k, side)

    def last_cols(side):
        need(("c", 4, side))
        need(("c", -4, side))
        to_sibling(4, side)

    def start(name):
        kind, k, side = name
        if kind == "c":
            device = to_xh if side else to_y(-k)
            send(cols_h, C.at[xh, y, core], name, device)
        else:
            device = to_xl if side else to_z(-k)
            send(rows_h, R.at[z, xl], name, device)

    for name in FIRST[:EARLY]:
        start(name)

    state = {}

    def g_share():
        loaded("cols")
        loaded("probes")
        phi, plo = split2(PR[...])
        state["phi"], state["both"] = phi, jnp.concatenate([phi, plo], axis=0)
        share = unpack(dot(C[xh, y, core], state["both"], ((1,), (1,))))
        state["mine"] = share
        GS[0, 0] = pack(share)
        for i, device in enumerate((to_xl, to_xh, to_diagonal)):
            send(GS.at[0, 0], GX.at[i], ("gx", i), device)
        for name in FIRST[EARLY:]:
            start(name)
        send(cols_h, C.at[xh, y, core], ("s", 0, 0), to_core)

    def g_x():
        for i in range(3):
            need(("gx", i))
        state["mine"] = state["mine"] + unpack(GX[0])
        state["theirs"] = unpack(GX[1]) + unpack(GX[2])
        GS[1, 0] = pack(state["mine"])
        GS[1, 1] = pack(state["theirs"])
        for k in (2, 1, -1):
            send(GS.at[1], place(("ga", k)), ("ga", k), to_z(-k))

    def g_add(names):
        for name in names:
            need(name)
            got = place(name)
            state["mine"] = state["mine"] + unpack(got[0])
            state["theirs"] = state["theirs"] + unpack(got[1])

    def g_z():
        g_add([("ga", k) for k in (1, -1, 2)])
        GS[2, 0] = pack(state["mine"])
        GS[2, 1] = pack(state["theirs"])
        for k in (4, -4):
            send(GS.at[2], place(("gb", k)), ("gb", k), to_z(-k))

    def g_y():
        g_add([("gb", k) for k in (4, -4)])
        GF[xh, y, core] = pack(state["mine"])
        GF[1 - xh, y, core] = pack(state["theirs"])
        for k in (1, -1, 2, -2):
            need(("c", k, 0))
        for k in (4, -4):
            b = GF.at[xh if k > 0 else 1 - xh, y, core]
            send(b, b, ("gf", k), to_y(-k))
        for k in (3, -3, 2, -2, 1, -1):
            send(GF.at[:, y, core], GF.at[:, y, core], ("gf", k), to_y(-k))

    def g_core():
        for k in (1, -1, 2, -2, 3, -3, 4, -4):
            need(("gf", k))
        send(GF.at[:, :, core], GF.at[:, :, core], ("gs", 0), to_core)

    def old_products(i):
        if i == 0:
            loaded("old")
        at = pl.ds(128 * i, 128)
        hi, lo = split2(OLD[at])
        PB[4 * i : 4 * i + 4] = pack(
            unpack(dot(hi, state["both"], ((1,), (1,)))) + dot(lo, state["phi"], ((1,), (1,)))
        ).reshape(4, 2, 16, 128)
        if i == 2:
            send(PB.at[:, 1 - xl], PX, ("px", 0), to_xl)

    def q_x():
        need(("px", 0))
        Q[...] = unpack(PB[:, xl]) + unpack(PX[...])
        QB[...] = pack(Q[...])
        for k in (6, 5, 4, -5, -4):
            s = 1 if k > 0 else -1
            send(QB.at[at_z(-k)], place(("qa", k)), ("qa", k), to_z(-(k - 3 * s)))
        for k in (2, -2, 1, -1):
            send(QB.at[at_z(-k)], place(("q", k)), ("q", k), to_z(-k))

    def q_far(s):
        total = Q[at_z(-3 * s)]
        for k in (4, 5, 6) if s > 0 else (-4, -5):
            need(("qa", k))
            total = total + unpack(place(("qa", k))[...])
        QS[0 if s > 0 else 1] = pack(total)
        send(QS.at[0 if s > 0 else 1], place(("q", 3 * s)), ("q", 3 * s), to_z(-3 * s))

    def q_sum():
        total = Q[z]
        for k in (1, -1, 2, -2, 3, -3):
            need(("q", k))
            total = total + unpack(place(("q", k))[...])
        state["old"] = total

    def mask():
        loaded("whitening")
        obs = lax.broadcasted_iota(jnp.int32, (768, 128), 0)
        first = COMP * lax.broadcasted_iota(jnp.int32, (768, 128), 1)
        keep = (obs >= first) & (obs < first + COMP)
        kept = jnp.sum(jnp.where(keep, mask_v[...].astype(F32), 0.0), axis=1, keepdims=True)
        Wm[...] = W[...] * kept.astype(BF)

    def turn(js):
        loaded("rows")
        reach = (1, -1, 2, -2, 3, -3) if 0 in js else (4, -4, 5, -5, 6, -6)
        for side in (0, 1):
            for k in reach:
                need(("r", k, side))
        need(("r", 0, 1))
        for j in js:
            pair = (z // 2 + j + 6) % 6
            block = R[pl.ds(2 * pair, 2)].reshape(128, 384)
            RT[:, pl.ds(pl.multiple_of(128 * pair, 128), 128)] = block.T

    def whiten(b):
        at, end = slice(256 * b, 256 * b + 256), 256 * b + 256
        WH[:, at] = dot(RT[:, :end], W[at, :end], ((1,), (1,))).astype(BF)

    def back(b):
        at = slice(256 * b, 256 * b + 256)
        hi, lo = split2(dot(WH[:, 256 * b :], Wm[256 * b :, at]))
        Y[:384, at] = hi
        Y[384:, at] = lo

    def gram(side, n):
        for k in (0, 1, -1, 2, -2, 3, -3, 4):
            need(("s", k, side))
        h = xh if side == 0 else 1 - xh
        at = pl.ds(256 * n, 256)
        left = Y[:, pl.ds(pl.multiple_of(384 * h, 128), 384)]
        both = dot(left, C[h, :, :, :, at].reshape(384, 256))
        new = OLD if side == 0 else new_o
        new[:, at] = OLD[:, at] + (both[:384] + both[384:])

    def products():
        need(("gs", 0))
        total = state["old"]
        at = pl.multiple_of(col * 16, 16)
        for first in (0, 384):
            total = total + unpack(dot(Y[pl.ds(first + at, 16), :], GF[...].reshape(768, 128)))
        prod_o[...] = total

    tasks = dict(
        g=g_share, g1=g_x, g2=g_z, g3=g_y, gs=g_core, p1=q_x, psum=q_sum, mask=mask, prod=products,
        c4_0=lambda: last_cols(0), c4_1=lambda: last_cols(1), p2a=lambda: q_far(1), p2b=lambda: q_far(-1),
        turnA=lambda: turn((0, 1, -1)), turnB=lambda: turn((2, -2, 3)),
    )
    for step in ORDER:
        if step in tasks:
            tasks[step]()
        elif isinstance(step, str):
            what, i = step[:-1], int(step[-1])
            many = dict(sold=old_products, white=whiten, back=back)
            if what in many:
                many[what](i)
            else:
                gram(0 if what == "gramA" else 1, i)
        else:
            came(step)
    for copy in sent:
        copy.wait_send()


def write_out(new_v, prod_v, new_h, prod_h, sems):
    copies = [pltpu.make_async_copy(prod_v, prod_h, sems.at[4])]
    for i in range(4):
        rows = pl.ds(96 * i, 96)
        copies.append(pltpu.make_async_copy(new_v.at[rows], new_h.at[rows], sems.at[i]))
    for copy in copies:
        copy.start()
    for copy in copies:
        copy.wait()


def body(design_rows, design_cols, whitening, epoch_mask, normal_old, probes):
    vmem = pl.BlockSpec(memory_space=pltpu.VMEM)
    hbm = pl.BlockSpec(memory_space=pltpu.HBM)
    new, products = pl.pallas_call(
        kernel,
        out_shape=(pltpu.VMEM((384, 1024), F32), pltpu.VMEM((16, 64), F32)),
        in_specs=[hbm, hbm, hbm, vmem, hbm, hbm],
        out_specs=(vmem, vmem),
        scratch_shapes=[
            pltpu.VMEM((NZ, 2, 32, 384), BF),
            pltpu.VMEM((384, 768), BF),
            pltpu.VMEM((2, NY, 2, 24, 1024), BF),
            pltpu.VMEM((768, 768), BF),
            pltpu.VMEM((768, 768), BF),
            pltpu.VMEM((384, 768), BF),
            pltpu.VMEM((768, 768), BF),
            pltpu.VMEM((384, 1024), F32),
            pltpu.VMEM((64, 1024), F32),
            pltpu.VMEM((NZ, 2, 16, 128), BF),
            pltpu.VMEM((NZ, 16, 128), BF),
            pltpu.VMEM((NZ, 16, 64), F32),
            pltpu.VMEM((NZ, 16, 128), BF),
            pltpu.VMEM((11, 16, 128), BF),
            pltpu.VMEM((2, 16, 128), BF),
            pltpu.VMEM((3, 24, 128), BF),
            pltpu.VMEM((3, 2, 24, 128), BF),
            pltpu.VMEM((5, 2, 24, 128), BF),
            pltpu.VMEM((2, NY, 2, 24, 128), BF),
            pltpu.SemaphoreType.DMA((128,)),
            pltpu.SemaphoreType.DMA((128,)),
            pltpu.SemaphoreType.DMA((5,)),
        ],
        compiler_params=pltpu.CompilerParams(
            collective_id=0, has_side_effects=True, vmem_limit_bytes=56 * 2**20
        ),
        name="normal_update",
    )(
        design_rows,
        design_cols,
        whitening,
        epoch_mask.reshape(1, 128),
        normal_old,
        probes.T,
    )
    return pl.pallas_call(
        write_out,
        out_shape=(
            jax.ShapeDtypeStruct((384, 1024), F32),
            jax.ShapeDtypeStruct((16, 64), F32),
        ),
        in_specs=[vmem, vmem],
        out_specs=(hbm, hbm),
        scratch_shapes=[pltpu.SemaphoreType.DMA((5,))],
        compiler_params=pltpu.CompilerParams(vmem_limit_bytes=4 * 2**20),
        name="write_out",
    )(new, products)


def solution(mesh):
    placed = (P("col", "row"), P("row", "col"), P(), P(), P("row", "col"), P("col", None))
    return jax.shard_map(
        body,
        mesh=mesh,
        in_specs=placed,
        out_specs=(P("row", "col"), P(("row", "col"), None)),
        check_vma=False,
    )
```

time: 121 us -> 44.5 us (0.37)
  the two profiles are of different devices: /device:TPU:8 before, /device:TPU:1 now
where the time goes in v3:
time: 44.5 us; the launch traced here: 44.3 us
  Pallas kernels  43.7 us (98%)
  between operations  0.64 us (1%)
    pallas_call x1, Pallas kernels, body(): pl.pallas_call(kernel, out_shape=(pltpu.VMEM((384, 1024), F32), pltpu.VME...  42.5 us
    pallas_call x1, Pallas kernels, body(): pl.pallas_call(write_out, out_shape=(jax.ShapeDtypeStruct((384, 1024), F3...  1.18 us

profile of v3, /device:TPU:1, one launch (start us, length us, event | category | flops | bytes accessed | tf_op | source)
XLA Modules:
  0.0 44.3 jit_solution(3982065386389532058)
XLA Ops:
  0.6 42.5 %normal_update.1 = (f32[384,1024]{1,0:T(8,128)S(1)}, f32[16,64]{1,0:T(8,128)S(1)}) custom-call(bf16[32,384]{1,0:T(8,128)(2,1)} %rows_h.1, bf16[24,1024]{1,0:T(8,128)(2,1)} %cols_h.1, bf16[768,768]{1,0:T(8,128)(2,1)} %w_h.1, s32[1,128]{1,0:T(1,128)} %bitcast.3, f32[384,1024]{1,0:T(8,128)} %old_h.1, f32[64,1024]{1,0:T(8,128)} %bitcast.2), custom_call_target="tpu_custom_call" | custom-call | tf_op jit(solution)/shard_map/normal_update/pallas_call | solution.py:401
  43.1 1.2 %write_out.1 = (f32[384,1024]{1,0:T(8,128)}, f32[16,64]{1,0:T(8,128)}) custom-call(f32[384,1024]{1,0:T(8,128)S(1)} %get-tuple-element.4.new_v, f32[16,64]{1,0:T(8,128)S(1)} %get-tuple-element.5.prod_v), custom_call_target="tpu_custom_call" | custom-call | tf_op jit(solution)/shard_map/write_out/pallas_call | solution.py:442

commit v4 on v3

--- a/solution.py
+++ b/solution.py
@@ -56,8 +56,8 @@
 
 
 def kernel(
-    rows_h, cols_h, w_h, mask_v, old_h, prob_h, new_o, prod_o,
-    R, RT, C, W, Wm, WH, Y, OLD, PR, PB, PX, Q, QB, QR, QS, GX, GS, GZ, GF, ss, rs, ls,
+    rows_h, cols_h, w_h, mask_h, old_h, prob_h, new_o, prod_o,
+    R, RT, C, W, Wm, WH, Y, OLD, PR, PB, PX, Q, QB, QR, QS, GX, GS, GZ, GF, MASK, ss, rs, ls,
 ):
     row, col = lax.axis_index("row"), lax.axis_index("col")
     core, y, xh = row % 2, (row // 2) % NY, row // (2 * NY)
@@ -94,6 +94,7 @@
                 ("cols", cols_h, C.at[xh, y, core]),
                 ("probes", prob_h, PR),
                 ("rows", rows_h, R.at[z, xl]),
+                ("mask", mask_h, MASK),
                 ("whitening", w_h, W),
                 ("old", old_h, OLD),
             )
@@ -101,9 +102,31 @@
     }
     for load in loads.values():
         load.start()
+
+    sems, sent, seen, state = Names(), [], set(), {}
+
+    def loaded(name):
+        if name not in seen:
+            seen.add(name)
+            loads[name].wait()
+
+    loaded("cols")
+    loaded("probes")
+    phi, plo = split2(PR[...])
+    state["phi"], state["both"] = phi, jnp.concatenate([phi, plo], axis=0)
+    state["mine"] = unpack(dot(C[xh, y, core], state["both"], ((1,), (1,))))
+    GS[0, 0] = pack(state["mine"])
+
+    def mask():
+        loaded("mask")
+        loaded("whitening")
+        obs = lax.broadcasted_iota(jnp.int32, (768, 128), 0)
+        first = COMP * lax.broadcasted_iota(jnp.int32, (768, 128), 1)
+        keep = (obs >= first) & (obs < first + COMP)
+        kept = jnp.sum(jnp.where(keep, MASK[...].astype(F32), 0.0), axis=1, keepdims=True)
+        Wm[...] = W[...] * kept.astype(BF)
+
     pl.semaphore_wait(barrier, len(others))
-
-    sems, sent, seen = Names(), [], set()
 
     def send(src, dst, name, device):
         copy = pltpu.make_async_remote_copy(
@@ -114,13 +137,8 @@
             device_id=device,
             device_id_type=MESH,
         )
-        copy.start()
+        copy.start(priority=0)
         sent.append(copy)
-
-    def loaded(name):
-        if name not in seen:
-            seen.add(name)
-            loads[name].wait()
 
     def place(name):
         kind, k, *side = name
@@ -141,7 +159,7 @@
                 return GF.at[xh if k > 0 else 1 - xh, at_y(k), core]
             return GF.at[:, at_y(k), core]
         if kind == "gs":
-            return GF.at[:, :, 1 - core]
+            return GF.at[:, at_y(k), 1 - core]
         if kind == "px":
             return PX
         if kind == "qa":
@@ -222,16 +240,7 @@
     for name in FIRST[:EARLY]:
         start(name)
 
-    state = {}
-
     def g_share():
-        loaded("cols")
-        loaded("probes")
-        phi, plo = split2(PR[...])
-        state["phi"], state["both"] = phi, jnp.concatenate([phi, plo], axis=0)
-        share = unpack(dot(C[xh, y, core], state["both"], ((1,), (1,))))
-        state["mine"] = share
-        GS[0, 0] = pack(share)
         for i, device in enumerate((to_xl, to_xh, to_diagonal)):
             send(GS.at[0, 0], GX.at[i], ("gx", i), device)
         for name in FIRST[EARLY:]:
@@ -275,9 +284,13 @@
             send(GF.at[:, y, core], GF.at[:, y, core], ("gf", k), to_y(-k))
 
     def g_core():
-        for k in (1, -1, 2, -2, 3, -3, 4, -4):
-            need(("gf", k))
-        send(GF.at[:, :, core], GF.at[:, :, core], ("gs", 0), to_core)
+        for k in (0, 1, -1, 2, -2, 3, -3, 4):
+            if k:
+                need(("gf", k))
+            if k == 4:
+                need(("gf", -4))
+            b = GF.at[:, at_y(k), core]
+            send(b, b, ("gs", k), to_core)
 
     def old_products(i):
         if i == 0:
@@ -314,14 +327,6 @@
             need(("q", k))
             total = total + unpack(place(("q", k))[...])
         state["old"] = total
-
-    def mask():
-        loaded("whitening")
-        obs = lax.broadcasted_iota(jnp.int32, (768, 128), 0)
-        first = COMP * lax.broadcasted_iota(jnp.int32, (768, 128), 1)
-        keep = (obs >= first) & (obs < first + COMP)
-        kept = jnp.sum(jnp.where(keep, mask_v[...].astype(F32), 0.0), axis=1, keepdims=True)
-        Wm[...] = W[...] * kept.astype(BF)
 
     def turn(js):
         loaded("rows")
@@ -356,7 +361,8 @@
         new[:, at] = OLD[:, at] + (both[:384] + both[384:])
 
     def products():
-        need(("gs", 0))
+        for k in (0, 1, -1, 2, -2, 3, -3, 4):
+            need(("gs", k))
         total = state["old"]
         at = pl.multiple_of(col * 16, 16)
         for first in (0, 384):
@@ -401,7 +407,7 @@
     new, products = pl.pallas_call(
         kernel,
         out_shape=(pltpu.VMEM((384, 1024), F32), pltpu.VMEM((16, 64), F32)),
-        in_specs=[hbm, hbm, hbm, vmem, hbm, hbm],
+        in_specs=[hbm] * 6,
         out_specs=(vmem, vmem),
         scratch_shapes=[
             pltpu.VMEM((NZ, 2, 32, 384), BF),
@@ -423,9 +429,10 @@
             pltpu.VMEM((3, 2, 24, 128), BF),
             pltpu.VMEM((5, 2, 24, 128), BF),
             pltpu.VMEM((2, NY, 2, 24, 128), BF),
+            pltpu.VMEM((1, 128), jnp.int32),
             pltpu.SemaphoreType.DMA((128,)),
             pltpu.SemaphoreType.DMA((128,)),
-            pltpu.SemaphoreType.DMA((5,)),
+            pltpu.SemaphoreType.DMA((6,)),
         ],
         compiler_params=pltpu.CompilerParams(
             collective_id=0, has_side_effects=True, vmem_limit_bytes=56 * 2**20

time: 44.5 us -> 43.7 us (0.982)
  Pallas kernels: 43.7 us -> 42.9 us
    pallas_call x1, Pallas kernels: 42.5 us -> 41.7 us  [body(): pl.pallas_call(kernel, out_shape=(pltpu.VMEM((384, 1024), F32), pltpu.VME...]
where the time goes in v4:
time: 43.7 us; the launch traced here: 43.5 us
  Pallas kernels  42.9 us (98%)
  between operations  0.64 us (1%)
    pallas_call x1, Pallas kernels, body(): pl.pallas_call(kernel, out_shape=(pltpu.VMEM((384, 1024), F32), pltpu.VME...  41.7 us
    pallas_call x1, Pallas kernels, body(): pl.pallas_call(write_out, out_shape=(jax.ShapeDtypeStruct((384, 1024), F3...  1.18 us

profile of v4, /device:TPU:1, one launch (start us, length us, event | category | flops | bytes accessed | tf_op | source)
XLA Modules:
  0.0 43.5 jit_solution(2469642626486372494)
XLA Ops:
  0.6 41.7 %normal_update.1 = (f32[384,1024]{1,0:T(8,128)S(1)}, f32[16,64]{1,0:T(8,128)S(1)}) custom-call(bf16[32,384]{1,0:T(8,128)(2,1)} %rows_h.1, bf16[24,1024]{1,0:T(8,128)(2,1)} %cols_h.1, bf16[768,768]{1,0:T(8,128)(2,1)} %w_h.1, s32[1,128]{1,0:T(1,128)} %bitcast.3, f32[384,1024]{1,0:T(8,128)} %old_h.1, f32[64,1024]{1,0:T(8,128)} %bitcast.2), custom_call_target="tpu_custom_call" | custom-call | tf_op jit(solution)/shard_map/normal_update/pallas_call | solution.py:407
  42.3 1.2 %write_out.1 = (f32[384,1024]{1,0:T(8,128)}, f32[16,64]{1,0:T(8,128)}) custom-call(f32[384,1024]{1,0:T(8,128)S(1)} %get-tuple-element.4.new_v, f32[16,64]{1,0:T(8,128)S(1)} %get-tuple-element.5.prod_v), custom_call_target="tpu_custom_call" | custom-call | tf_op jit(solution)/shard_map/write_out/pallas_call | solution.py:449

commit v5 on v4

--- a/solution.py
+++ b/solution.py
@@ -36,22 +36,21 @@
 
 
 ROWS_ACROSS, ROWS_DIRECT = (3, -3), (2, -2, 1, -1)
-COLS_ACROSS, COLS_DIRECT = (2, -2), (1, -1)
+COLS_ACROSS, COLS_DIRECT = (2, -2, 1, -1), ()
 FIRST = (
-    ("r", 1, 0), ("r", -3, 0), ("r", 3, 0), ("r", -2, 0), ("c", 2, 0), ("c", 1, 0),
-    ("c", -2, 0), ("r", 0, 1), ("r", 2, 0), ("r", -1, 0), ("c", 0, 1), ("c", -1, 0),
+    ("c", -1, 0), ("r", 3, 0), ("r", -3, 0), ("r", 1, 0), ("c", 1, 0), ("r", 2, 0),
+    ("r", 0, 1), ("c", -2, 0), ("r", -2, 0), ("c", 2, 0), ("c", 0, 1), ("r", -1, 0),
 )
-EARLY = 9
+EARLY = 10
 ORDER = (
-    "g", "mask", "sold0", ("r", 0, 1), "sold1", "sold2",
-    "g1", ("c", 1, 0), ("c", -2, 0), ("r", 3, 0), ("c", 2, 0), ("c", -1, 0),
-    ("r", -3, 0), ("c", 0, 1), "p1", "g2", ("c", -3, 0), ("r", 3, 1),
-    ("c", -2, 1), ("c", 3, 0), ("c", 1, 1), ("c", -1, 1), ("r", -3, 1), ("c", 2, 1),
-    "c4_0", "p2b", "turnA", "p2a", ("c", -3, 1), "g3",
-    "c4_1", ("c", 3, 1), "turnB", "white0", "white1", "white2",
-    "back2", "back1", "back0", "gramA0", "gramA1", "gramA2",
-    "gramA3", "gramB0", "gs", "gramB1", "gramB2", "gramB3",
-    "psum", "prod",
+    "g", "mask", "sold0", ("c", -1, 0), ("r", 0, 1), ("c", 1, 0),
+    "sold1", "sold2", "g1", ("c", -2, 0), ("c", 2, 0), ("r", 3, 0),
+    ("r", -3, 0), "g2", ("c", 0, 1), ("c", 1, 1), ("c", -1, 1), "p1",
+    ("c", -3, 0), "c4_0", ("c", 3, 0), ("c", -2, 1), ("r", 3, 1), ("c", 2, 1),
+    ("r", -3, 1), "turnA", "p2b", "p2a", "g3", ("c", -3, 1),
+    ("c", 3, 1), "c4_1", "turnB", "white0", "white1", "white2",
+    "back2", "back1", "back0", "gs", "gram0", "gram1",
+    "gram2", "gram3", "psum", "prod",
 )
 
 
@@ -350,15 +349,13 @@
         Y[:384, at] = hi
         Y[384:, at] = lo
 
-    def gram(side, n):
-        for k in (0, 1, -1, 2, -2, 3, -3, 4):
-            need(("s", k, side))
-        h = xh if side == 0 else 1 - xh
-        at = pl.ds(256 * n, 256)
-        left = Y[:, pl.ds(pl.multiple_of(384 * h, 128), 384)]
-        both = dot(left, C[h, :, :, :, at].reshape(384, 256))
-        new = OLD if side == 0 else new_o
-        new[:, at] = OLD[:, at] + (both[:384] + both[384:])
+    def gram(n):
+        for side in (0, 1):
+            for k in (0, 1, -1, 2, -2, 3, -3, 4):
+                need(("s", k, side))
+        at = slice(256 * n, 256 * n + 256)
+        both = dot(Y[...], C[:, :, :, :, at].reshape(768, 256))
+        new_o[:, at] = OLD[:, at] + (both[:384] + both[384:])
 
     def products():
         for k in (0, 1, -1, 2, -2, 3, -3, 4):
@@ -379,11 +376,7 @@
             tasks[step]()
         elif isinstance(step, str):
             what, i = step[:-1], int(step[-1])
-            many = dict(sold=old_products, white=whiten, back=back)
-            if what in many:
-                many[what](i)
-            else:
-                gram(0 if what == "gramA" else 1, i)
+            dict(sold=old_products, white=whiten, back=back, gram=gram)[what](i)
         else:
             came(step)
     for copy in sent:

time: 43.7 us -> 42.7 us (0.977)
  Pallas kernels: 42.9 us -> 41.9 us
    pallas_call x1, Pallas kernels: 41.7 us -> 40.7 us  [body(): pl.pallas_call(kernel, out_shape=(pltpu.VMEM((384, 1024), F32), pltpu.VME...]
where the time goes in v5:
time: 42.7 us; the launch traced here: 42.6 us
  Pallas kernels  41.9 us (98%)
  between operations  0.64 us (1%)
    pallas_call x1, Pallas kernels, body(): pl.pallas_call(kernel, out_shape=(pltpu.VMEM((384, 1024), F32), pltpu.VME...  40.7 us
    pallas_call x1, Pallas kernels, body(): pl.pallas_call(write_out, out_shape=(jax.ShapeDtypeStruct((384, 1024), F3...  1.18 us

profile of v5, /device:TPU:1, one launch (start us, length us, event | category | flops | bytes accessed | tf_op | source)
XLA Modules:
  0.0 42.6 jit_solution(815596342686267558)
XLA Ops:
  0.6 40.7 %normal_update.1 = (f32[384,1024]{1,0:T(8,128)S(1)}, f32[16,64]{1,0:T(8,128)S(1)}) custom-call(bf16[32,384]{1,0:T(8,128)(2,1)} %rows_h.1, bf16[24,1024]{1,0:T(8,128)(2,1)} %cols_h.1, bf16[768,768]{1,0:T(8,128)(2,1)} %w_h.1, s32[1,128]{1,0:T(1,128)} %bitcast.3, f32[384,1024]{1,0:T(8,128)} %old_h.1, f32[64,1024]{1,0:T(8,128)} %bitcast.2), custom_call_target="tpu_custom_call" | custom-call | tf_op jit(solution)/shard_map/normal_update/pallas_call | solution.py:400
  41.4 1.2 %write_out.1 = (f32[384,1024]{1,0:T(8,128)}, f32[16,64]{1,0:T(8,128)}) custom-call(f32[384,1024]{1,0:T(8,128)S(1)} %get-tuple-element.4.new_v, f32[16,64]{1,0:T(8,128)S(1)} %get-tuple-element.5.prod_v), custom_call_target="tpu_custom_call" | custom-call | tf_op jit(solution)/shard_map/write_out/pallas_call | solution.py:442

commit v6 on v5

--- a/solution.py
+++ b/solution.py
@@ -55,7 +55,7 @@
 
 
 def kernel(
-    rows_h, cols_h, w_h, mask_h, old_h, prob_h, new_o, prod_o,
+    rows_h, cols_h, w_h, mask_h, old_h, prob_h, new_o, left_o, old_o, g_o,
     R, RT, C, W, Wm, WH, Y, OLD, PR, PB, PX, Q, QB, QR, QS, GX, GS, GZ, GF, MASK, ss, rs, ls,
 ):
     row, col = lax.axis_index("row"), lax.axis_index("col")
@@ -358,13 +358,13 @@
         new_o[:, at] = OLD[:, at] + (both[:384] + both[384:])
 
     def products():
+        at = pl.multiple_of(col * 16, 16)
+        left_o[:16] = Y[pl.ds(at, 16), :]
+        left_o[16:] = Y[pl.ds(384 + at, 16), :]
+        old_o[...] = state["old"]
         for k in (0, 1, -1, 2, -2, 3, -3, 4):
             need(("gs", k))
-        total = state["old"]
-        at = pl.multiple_of(col * 16, 16)
-        for first in (0, 384):
-            total = total + unpack(dot(Y[pl.ds(first + at, 16), :], GF[...].reshape(768, 128)))
-        prod_o[...] = total
+        g_o[...] = GF[...].reshape(768, 128)
 
     tasks = dict(
         g=g_share, g1=g_x, g2=g_z, g3=g_y, gs=g_core, p1=q_x, psum=q_sum, mask=mask, prod=products,
@@ -383,13 +383,17 @@
         copy.wait_send()
 
 
-def write_out(new_v, prod_v, new_h, prod_h, sems):
-    copies = [pltpu.make_async_copy(prod_v, prod_h, sems.at[4])]
+def write_out(new_v, left_v, old_v, g_v, new_h, prod_h, prod_v, sems):
+    copies = []
     for i in range(4):
         rows = pl.ds(96 * i, 96)
         copies.append(pltpu.make_async_copy(new_v.at[rows], new_h.at[rows], sems.at[i]))
     for copy in copies:
         copy.start()
+    both = unpack(dot(left_v[...], g_v[...]))
+    prod_v[...] = old_v[...] + both[:16] + both[16:]
+    copies.append(pltpu.make_async_copy(prod_v, prod_h, sems.at[4]))
+    copies[4].start()
     for copy in copies:
         copy.wait()
 
@@ -397,11 +401,16 @@
 def body(design_rows, design_cols, whitening, epoch_mask, normal_old, probes):
     vmem = pl.BlockSpec(memory_space=pltpu.VMEM)
     hbm = pl.BlockSpec(memory_space=pltpu.HBM)
-    new, products = pl.pallas_call(
+    parts = pl.pallas_call(
         kernel,
-        out_shape=(pltpu.VMEM((384, 1024), F32), pltpu.VMEM((16, 64), F32)),
+        out_shape=(
+            pltpu.VMEM((384, 1024), F32),
+            pltpu.VMEM((32, 768), BF),
+            pltpu.VMEM((16, 64), F32),
+            pltpu.VMEM((768, 128), BF),
+        ),
         in_specs=[hbm] * 6,
-        out_specs=(vmem, vmem),
+        out_specs=(vmem,) * 4,
         scratch_shapes=[
             pltpu.VMEM((NZ, 2, 32, 384), BF),
             pltpu.VMEM((384, 768), BF),
@@ -445,12 +454,12 @@
             jax.ShapeDtypeStruct((384, 1024), F32),
             jax.ShapeDtypeStruct((16, 64), F32),
         ),
-        in_specs=[vmem, vmem],
+        in_specs=[vmem] * 4,
         out_specs=(hbm, hbm),
-        scratch_shapes=[pltpu.SemaphoreType.DMA((5,))],
+        scratch_shapes=[pltpu.VMEM((16, 64), F32), pltpu.SemaphoreType.DMA((5,))],
         compiler_params=pltpu.CompilerParams(vmem_limit_bytes=4 * 2**20),
         name="write_out",
-    )(new, products)
+    )(*parts)
 
 
 def solution(mesh):

time: 42.7 us -> 42.4 us (level)
  no operation moved by 1% of the time
where the time goes in v6:
time: 42.4 us; the launch traced here: 42.3 us
  Pallas kernels  41.7 us (98%)
  between operations  0.64 us (2%)
    pallas_call x1, Pallas kernels, body(): pl.pallas_call(kernel, out_shape=(pltpu.VMEM((384, 1024), F32), pltpu.VME...  40.5 us
    pallas_call x1, Pallas kernels, body(): pl.pallas_call(write_out, out_shape=(jax.ShapeDtypeStruct((384, 1024), F3...  1.18 us

profile of v6, /device:TPU:1, one launch (start us, length us, event | category | flops | bytes accessed | tf_op | source)
XLA Modules:
  0.0 42.3 jit_solution(9409907366787617423)
XLA Ops:
  0.6 40.5 %normal_update.1 = (f32[384,1024]{1,0:T(8,128)S(1)}, bf16[32,768]{1,0:T(8,128)(2,1)S(1)}, f32[16,64]{1,0:T(8,128)S(1)}, bf16[768,128]{1,0:T(8,128)(2,1)S(1)}) custom-call(bf16[32,384]{1,0:T(8,128)(2,1)} %rows_h.1, bf16[24,1024]{1,0:T(8,128)(2,1)} %cols_h.1, bf16[768,768]{1,0:T(8,128)(2,1)} %w_h.1, s32[1,128]{1,0:T(1,128)} %bitcast.3, f32[384,1024]{1,0:T(8,128)} %old_h.1, ...), custom_call_target="tpu_custom_call" | custom-call | tf_op jit(solution)/shard_map/normal_update/pallas_call | solution.py:404
  41.1 1.2 %write_out.1 = (f32[384,1024]{1,0:T(8,128)}, f32[16,64]{1,0:T(8,128)}) custom-call(f32[384,1024]{1,0:T(8,128)S(1)} %get-tuple-element.6.new_v, bf16[32,768]{1,0:T(8,128)(2,1)S(1)} %get-tuple-element.7.left_v, f32[16,64]{1,0:T(8,128)S(1)} %get-tuple-element.8.old_v, bf16[768,128]{1,0:T(8,128)(2,1)S(1)} %get-tuple-element.9.g_v), custom_call_target="tpu_custom_call" | custom-call | tf_op jit(solution)/shard_map/write_out/pallas_call | solution.py:451
